TPU v7x, 128 devices: a whole 4x4x4 slice. The times are simulated.
128 devices in a mesh: ax: 16 (over z, y_lo, core), rad: 8 (over x, y_hi).
Axes of the slice: x: 4, y: 4 (y_hi: 2, y_lo: 2; y = y_hi * 2 + y_lo), z: 4, core: 2. Of those that a mesh axis runs over, the one named last changes fastest.
Arguments:
- velocity: float32 [3, 128, 512, 1024], P(None, 'ax', 'rad'), may hold values from -6 to 6
- viscosity: float32 [128, 512, 1024], P('ax', 'rad'), may hold values from 0.05 to 0.5
- inv_dx: float32 [128], P('ax'), may hold values from 0.5 to 2
- inv_dr: float32 [512], P('rad'), may hold values from 0.5 to 2
- inv_rt: float32 [512], P('rad'), may hold values from 0.5 to 2
- az_inverse: float32 [1024, 1024], replicated, may hold values from -0.5 to 2.5
- rad_inverse: float32 [512, 512], replicated, may hold values from -0.5 to 2.5
Outputs:
- velocity_next: float32 [3, 128, 512, 1024], P(None, 'ax', 'rad')
All inputs are finite; a program needn't handle non-finite values.
Results may differ from a plain program's by a relative error of at most 0.0003.
Values sent between devices are 32-bit elements; how exact they have to be, the bound alone decides.
No kernel may reach another device: no remote copies, remote signals or barrier semaphores. Data moves between devices by JAX's collectives and lax.ppermute only.
A program may use at most 256 MiB of HBM per device.

v0:
```python
import jax
import jax.numpy as jnp
from jax import lax
from jax.sharding import PartitionSpec as P

COEF = 0.25


def padded_2(block, sides, width):
    for axis, dim in sides:
        count = lax.axis_size(axis)
        forward = [(i, i + 1) for i in range(count - 1)]
        backward = [(target, source) for source, target in forward]
        low = lax.ppermute(
            lax.slice_in_dim(block, block.shape[dim] - width, None, axis=dim), axis, forward
        )
        high = lax.ppermute(lax.slice_in_dim(block, 0, width, axis=dim), axis, backward)
        block = jnp.concatenate([low, block, high], axis=dim)
    return block


def tendency(padded, inv_dx, inv_dr, inv_rt):
    planes = padded.shape[1] - 4
    radial = padded.shape[2] - 4

    def shifted(step_a, step_r):
        return padded[:, 2 + step_a : 2 + step_a + planes, 2 + step_r : 2 + step_r + radial, :]

    centre = shifted(0, 0)
    vel = centre[:3]
    visc = centre[3]
    metric_x = inv_dx[:, None, None]
    metric_r = inv_dr[None, :, None]
    metric_t = inv_rt[None, :, None]

    def parts(metric, plus_one, minus_one, plus_two, minus_two):
        deriv = (
            metric * (8.0 * (plus_one[:3] - minus_one[:3]) - (plus_two[:3] - minus_two[:3])) / 12.0
        )
        upper = 0.5 * (visc + plus_one[3]) * (plus_one[:3] - vel)
        lower = 0.5 * (visc + minus_one[3]) * (vel - minus_one[:3])
        return (deriv, metric * metric * (upper - lower))

    deriv_x, diff_x = parts(metric_x, shifted(1, 0), shifted(-1, 0), shifted(2, 0), shifted(-2, 0))
    deriv_r, diff_r = parts(metric_r, shifted(0, 1), shifted(0, -1), shifted(0, 2), shifted(0, -2))
    deriv_t, diff_t = parts(
        metric_t,
        jnp.roll(centre, -1, axis=3),
        jnp.roll(centre, 1, axis=3),
        jnp.roll(centre, -2, axis=3),
        jnp.roll(centre, 2, axis=3),
    )
    advect = vel[0] * deriv_x + vel[1] * deriv_t + vel[2] * deriv_r
    return vel + COEF * (diff_x + diff_t + diff_r - advect)


def local(velocity, viscosity, inv_dx, inv_dr, inv_rt, az_inverse, rad_inverse):
    fields = jnp.concatenate([velocity, viscosity[None]], axis=0)
    padded = padded_2(fields, (("ax", 1), ("rad", 2)), 2)
    rhs = tendency(padded, inv_dx, inv_dr, inv_rt)

    def radial(field):
        return jnp.einsum("rk,cakt->cart", rad_inverse, field, precision=lax.Precision.HIGHEST)

    solved = jnp.einsum("cars,ts->cart", rhs, az_inverse, precision=lax.Precision.HIGHEST)
    return lax.all_to_all(
        radial(lax.all_to_all(solved, "rad", split_axis=3, concat_axis=2, tiled=True)),
        "rad",
        split_axis=2,
        concat_axis=3,
        tiled=True,
    )


def solution(mesh):
    placed = (
        P(None, "ax", "rad", None),
        P("ax", "rad", None),
        P("ax"),
        P("rad"),
        P("rad"),
        P(),
        P(),
    )
    return jax.shard_map(
        local, mesh=mesh, in_specs=placed, out_specs=P(None, "ax", "rad", None), check_vma=False
    )
```

profile of v0, /device:TPU:96, one launch (start us, length us, event | category | flops | bytes accessed | tf_op | source)
XLA Modules:
  0.0 418.2 jit_solution(3006121644179621851)
XLA Ops:
  0.0 0.0 copy-start
  0.0 0.0 copy-start.9
  0.0 0.0 copy-start.8
  0.0 0.0 copy-start.7
  0.0 0.0 copy-start.1
  0.0 0.0 copy-start.2
  0.0 5.0 %fusion.75 = (f32[4,2,64,1024]{3,2,1,0:T(8,128)}, f32[4,2,64,1024]{3,2,1,0:T(8,128)}) fusion(f32[3,8,64,1024]{3,2,1,0:T(8,128)} %param.7, f32[1,8,64,1024]{3,2,1,0:T(8,128)} %bitcast.69), kind=kLoop, calls=%fused_computation.109 | loop fusion | flops 1048576 | bytes 12582912 | tf_op jit(solution)/shard_map/concatenate | solution.py:58
  5.1 2.9 collective-permute-start
  8.0 1.9 collective-permute-start.1
  9.9 0.0 copy-done.9
  9.9 0.0 copy-done.8
  9.9 0.6 mul.188
  10.5 0.0 copy-done.7
  10.5 0.6 mul.197
  11.1 0.0 copy-done.1
  11.1 0.0 copy-done.2
  11.1 0.4 fusion.89
  11.5 0.0 copy-start.6
  11.5 0.0 copy-start.5
  11.5 2.0 fusion.91
  13.5 5.1 %fusion.2 = f32[4,8,64,1022]{3,2,1,0:T(8,128)} fusion(f32[3,8,64,1024]{3,2,1,0:T(8,128)S(1)} %copy-done.1, f32[1,8,64,1024]{3,2,1,0:T(8,128)S(1)} %bitcast.72), kind=kLoop, calls=%fused_computation.22 | loop fusion | flops 2093056 | bytes 16760832 | tf_op jit(solution)/shard_map/concatenate | solution.py:58
  18.7 5.8 %fusion = (f32[4,8,64,1023]{3,2,1,0:T(8,128)S(1)}, f32[4,8,64,1023]{3,2,1,0:T(8,128)}) fusion(f32[3,8,64,1024]{3,2,1,0:T(8,128)S(1)} %copy-done.1, f32[1,8,64,1024]{3,2,1,0:T(8,128)S(1)} %bitcast.73), kind=kLoop, calls=%fused_computation.20 | loop fusion | flops 4190208 | bytes 25149440 | tf_op jit(solution)/shard_map/concatenate | solution.py:58
  24.4 0.0 copy-start.3
  24.4 0.0 copy-done.6
  24.4 2.1 fusion.83
  26.6 1.7 copy-done.3
  28.3 2.9 multiply_bitcast_fusion.2
  31.2 21.0 %collective-permute-done = f32[4,2,64,1024]{3,2,1,0:T(8,128)S(1)} collective-permute-done((f32[4,2,64,1024]{3,2,1,0:T(8,128)}, f32[4,2,64,1024]{3,2,1,0:T(8,128)S(1)}, u32[]{:S(2)}, u32[]{:S(2)}) %collective-permute-start) | collective-permute-done | bytes 2097184 | tf_op jit(solution)/shard_map/ppermute | solution.py:17
  52.1 0.0 copy-start.4
  52.1 3.2 collective-permute-done.1
  55.3 1.4 pad_maximum_fusion.32
  56.7 1.3 collective-permute-start.2
  58.0 0.0 slice-start
  58.0 0.0 slice-start.1
  58.0 7.1 %collective-permute-start.3 = (f32[4,12,2,1024]{3,2,1,0:T(2,128)S(1)}, f32[4,12,2,1024]{3,2,1,0:T(2,128)}, u32[]{:S(2)}, u32[]{:S(2)}) collective-permute-start(f32[4,12,2,1024]{3,2,1,0:T(2,128)S(1)} %get-tuple-element.10), channel_id=1, source_target_pairs={{0,1},{1,2},{2,3},{3,4},{4,5},{5,6},{6,7},{8,9},{9,10},{10,11},{11... | collective-permute-start | bytes 1179656 | tf_op jit(solution)/shard_map/ppermute | solution.py:14
  65.1 0.0 copy-done.4
  65.1 8.6 %pad_maximum_fusion = (f32[4,10,64,1024]{3,2,1,0:T(8,128)}, f32[4,10,64,1024]{3,2,1,0:T(8,128)}) fusion(f32[4,2,64,1024]{3,2,1,0:T(8,128)S(1)} %collective-permute-done, f32[1,8,64,1024]{3,2,1,0:T(8,128)S(1)} %bitcast.75, f32[3,8,64,1024]{3,2,1,0:T(8,128)S(1)} %copy-done.1, f32[4,2,64,1024]{3,2,1,0:T(8,128)} %collective-permute-done.1), kind=kLoop, calls=%fused_computation.18 | loop fusion | flops 10485760 | bytes 33554432 | tf_op jit(solution)/shard_map/concatenate | solution.py:18
  73.6 0.0 collective-permute-done.2
  73.6 4.8 %collective-permute-done.3 = f32[4,12,2,1024]{3,2,1,0:T(2,128)} collective-permute-done((f32[4,12,2,1024]{3,2,1,0:T(2,128)S(1)}, f32[4,12,2,1024]{3,2,1,0:T(2,128)}, u32[]{:S(2)}, u32[]{:S(2)}) %collective-permute-start.3) | collective-permute-done | bytes 393248 | tf_op jit(solution)/shard_map/ppermute | solution.py:14
  78.4 0.0 copy-done.5
  78.4 0.0 slice-done
  78.4 0.0 slice-done.1
  78.5 6.2 %fusion.79 = (f32[8,64,1024]{2,1,0:T(8,128)}, f32[8,64,1024]{2,1,0:T(8,128)}, f32[8,64,1024]{2,1,0:T(8,128)}, f32[8,64,1024]{2,1,0:T(8,128)}, f32[8,64,1024]{2,1,0:T(8,128)}) fusion(f32[8,64,1024]{2,1,0:T(8,128)S(1)} %copy-done.2, f32[4,12,2,1024]{3,2,1,0:T(2,128)S(1)} %collective-permute-done.2, f32[4,2,64,1024]{3,2,1,0:T(8,128)} %copy-done.4, ...), kind=kLoop, calls=%fused_computation.115 | loop fusion | flops 12058624 | bytes 34340864 | tf_op jit(solution)/shard_map/mul | solution.py:40
  84.6 68.5 %fusion.11 = f32[3,8,64,1024]{3,2,1,0:T(8,128)} fusion(f32[3,8,64,1024]{3,2,1,0:T(8,128)} %param.7, f32[4,12,2,1024]{3,2,1,0:T(2,128)} %collective-permute-done.3, f32[4,2,64,1024]{3,2,1,0:T(8,128)} %copy-done.4, f32[4,2,64,1024]{3,2,1,0:T(8,128)} %collective-permute-done.1, f32[1,8,64,1024]{3,2,1,0:T(8,128)S(1)} %bitcast.77, ...), kind=kOutput, calls=%fused_computation.32 | convolution fusion | flops 19428016128 | bytes 97257024 | tf_op jit(solution)/shard_map/cars,ts->cart/dot_general | solution.py:65
  153.1 9.8 %copy.22 = f32[3,8,64,1024]{2,1,0,3:T(8,128)} copy(f32[3,8,64,1024]{3,2,1,0:T(8,128)} %fusion.11) | data formatting | bytes 12582912 | tf_op jit(solution)/shard_map/cars,ts->cart/dot_general | solution.py:65
  162.9 12.6 %reshape.26 = f32[8,1,196608]{2,1,0:T(1,128)} reshape(f32[1024,3,8,64]{3,2,1,0:T(8,128)} %bitcast.78) | data formatting | bytes 12582912
  175.5 81.7 %all_to_all.36 = f32[8,1,196608]{2,1,0:T(1,128)} all-to-all(f32[8,1,196608]{2,1,0:T(1,128)} %reshape.26), channel_id=1, replica_groups=mesh['ax'=16,'rad'=8] {'rad'}, dimensions={0} | all-to-all | bytes 12582912 | tf_op jit(solution)/shard_map/all_to_all | solution.py:67
  257.2 0.6 broadcast.46
  257.8 19.5 %reduce = f32[8,196608]{1,0:T(8,128)} reduce(f32[8,1,196608]{2,1,0:T(1,128)} %all_to_all.36, f32[]{:T(128)} %broadcast.46), dimensions={1}, to_apply=%all_to_all.26.reduce_sub_computation | reduce | bytes 12582916 | tf_op jit(solution)/shard_map/all_to_all | solution.py:67
  277.4 12.2 %reshape.27 = f32[1024,3,8,64]{3,2,1,0:T(8,128)} reshape(f32[8,196608]{1,0:T(8,128)} %reduce) | data formatting | bytes 12582912
  289.6 9.8 %copy.24 = f32[3,8,8,64,128]{4,3,2,1,0:T(8,128)} copy(f32[3,8,8,64,128]{3,1,0,4,2:T(8,128)} %bitcast.79) | data formatting | bytes 12582912 | tf_op jit(solution)/shard_map/all_to_all | solution.py:67
  299.3 0.0 copy-done
  299.3 23.0 %convolution_bitcast_fusion = f32[3,8,512,128]{2,3,1,0:T(8,128)} fusion(f32[3,8,512,128]{3,2,1,0:T(8,128)} %bitcast.83, f32[512,512]{1,0:T(8,128)S(1)} %copy-done), kind=kOutput, calls=%fused_computation.107 | convolution fusion | flops 9663676416 | bytes 13631488 | tf_op jit(solution)/shard_map/rk,cakt->cart/dot_general | solution.py:63
  322.3 6.6 %copy.26 = f32[3,8,512,128]{3,1,0,2:T(8,128)} copy(f32[3,8,512,128]{2,3,1,0:T(8,128)} %convolution_bitcast_fusion) | data formatting | bytes 12582912 | tf_op jit(solution)/shard_map/rk,cakt->cart/transpose | solution.py:63
  328.8 76.0 %all_to_all.37 = f32[3,8,512,128]{3,1,0,2:T(8,128)S(1)} all-to-all(f32[3,8,512,128]{3,1,0,2:T(8,128)} %copy.26), channel_id=1, replica_groups=mesh['ax'=16,'rad'=8] {'rad'}, dimensions={2} | all-to-all | bytes 12582912 | tf_op jit(solution)/shard_map/all_to_all | solution.py:66
  404.9 6.3 %copy.28 = f32[3,8,64,8,128]{4,3,2,1,0:T(8,128)} copy(f32[3,8,64,8,128]{4,1,0,2,3:T(8,128)S(1)} %bitcast.82) | data formatting | bytes 12582912 | tf_op jit(solution)/shard_map/all_to_all | solution.py:66
  411.2 7.1 %all_to_all.33 = f32[3,8,64,1024]{3,2,1,0:T(8,128)} reshape(f32[3,8,64,8,128]{4,3,2,1,0:T(8,128)} %copy.28) | data formatting | bytes 12582912 | tf_op jit(solution)/shard_map/all_to_all | solution.py:66
  (2 shorter events, 0.0 us)
Async XLA Ops:
  0.0 299.3 %copy-start = (f32[512,512]{1,0:T(8,128)S(1)}, f32[512,512]{1,0:T(8,128)}, u32[]{:S(2)}) copy-start(f32[512,512]{1,0:T(8,128)} %param.13) | copy-start | bytes 3145732
  0.0 9.9 %copy-start.9 = (f32[8]{0:T(128)S(1)}, f32[8]{0:T(128)}, u32[]{:S(2)}) copy-start(f32[8]{0:T(128)} %param.9) | copy-start | bytes 100
  0.0 9.9 %copy-start.8 = (f32[64]{0:T(128)S(1)}, f32[64]{0:T(128)}, u32[]{:S(2)}) copy-start(f32[64]{0:T(128)} %param.11) | copy-start | bytes 772
  0.0 10.5 %copy-start.7 = (f32[64]{0:T(128)S(1)}, f32[64]{0:T(128)}, u32[]{:S(2)}) copy-start(f32[64]{0:T(128)} %param.10) | copy-start | bytes 772
  0.0 11.1 %copy-start.1 = (f32[3,8,64,1024]{3,2,1,0:T(8,128)S(1)}, f32[3,8,64,1024]{3,2,1,0:T(8,128)}, u32[]{:S(2)}) copy-start(f32[3,8,64,1024]{3,2,1,0:T(8,128)} %param.7) | copy-start | bytes 18874372
  0.0 11.1 %copy-start.2 = (f32[8,64,1024]{2,1,0:T(8,128)S(1)}, f32[8,64,1024]{2,1,0:T(8,128)}, u32[]{:S(2)}) copy-start(f32[8,64,1024]{2,1,0:T(8,128)} %param.8) | copy-start | bytes 6291460
  5.1 47.1 %collective-permute-start = (f32[4,2,64,1024]{3,2,1,0:T(8,128)}, f32[4,2,64,1024]{3,2,1,0:T(8,128)S(1)}, u32[]{:S(2)}, u32[]{:S(2)}) collective-permute-start(f32[4,2,64,1024]{3,2,1,0:T(8,128)} %get-tuple-element.20), channel_id=1, source_target_pairs={{8,0},{16,8},{24,16},{32,24},{40,32},{48,40},{56,48},{64,56},{72,6... | collective-permute-start | bytes 6291464 | tf_op jit(solution)/shard_map/ppermute | solution.py:17
  8.0 47.3 %collective-permute-start.1 = (f32[4,2,64,1024]{3,2,1,0:T(8,128)}, f32[4,2,64,1024]{3,2,1,0:T(8,128)}, u32[]{:S(2)}, u32[]{:S(2)}) collective-permute-start(f32[4,2,64,1024]{3,2,1,0:T(8,128)} %get-tuple-element.19), channel_id=1, source_target_pairs={{0,8},{8,16},{16,24},{24,32},{32,40},{40,48},{48,56},{56,64},{64,7... | collective-permute-start | bytes 6291464 | tf_op jit(solution)/shard_map/ppermute | solution.py:14
  11.5 12.9 %copy-start.6 = (f32[4,8,64,1]{3,2,1,0:T(8,128)}, f32[4,8,64,1]{3,2,1,0:T(8,128)S(1)}, u32[]{:S(2)}) copy-start(f32[4,8,64,1]{3,2,1,0:T(8,128)S(1)} %get-tuple-element.13) | copy-start | bytes 24580
  11.5 66.9 %copy-start.5 = (f32[4,8,64,1]{3,2,1,0:T(8,128)}, f32[4,8,64,1]{3,2,1,0:T(8,128)S(1)}, u32[]{:S(2)}) copy-start(f32[4,8,64,1]{3,2,1,0:T(8,128)S(1)} %get-tuple-element.14) | copy-start | bytes 24580
  24.4 3.9 copy-start.3
  52.1 13.0 %copy-start.4 = (f32[4,2,64,1024]{3,2,1,0:T(8,128)}, f32[4,2,64,1024]{3,2,1,0:T(8,128)S(1)}, u32[]{:S(2)}) copy-start(f32[4,2,64,1024]{3,2,1,0:T(8,128)S(1)} %collective-permute-done) | copy-start | bytes 6291460
  56.7 16.9 %collective-permute-start.2 = (f32[4,12,2,1024]{3,2,1,0:T(2,128)S(1)}, f32[4,12,2,1024]{3,2,1,0:T(2,128)S(1)}, u32[]{:S(2)}, u32[]{:S(2)}) collective-permute-start(f32[4,12,2,1024]{3,2,1,0:T(2,128)S(1)} %get-tuple-element.9), channel_id=1, source_target_pairs={{1,0},{2,1},{3,2},{4,3},{5,4},{6,5},{7,6},{9,8},{10,9},{11,10},{12... | collective-permute-start | bytes 1179656 | tf_op jit(solution)/shard_map/ppermute | solution.py:17
  58.0 20.5 %slice-start = ((s8[8388608]{0:T(1024)(128)(4,1)}), s8[4194304]{0:T(1024)(128)(4,1)S(1)}, s32[]{:S(2)}) async-start(s8[8388608]{0:T(1024)(128)(4,1)} %bitcast.80), calls=%async_computation.2 | async-start | bytes 8388608
  58.0 20.4 %slice-start.1 = ((s8[8388608]{0:T(1024)(128)(4,1)}), s8[4194304]{0:T(1024)(128)(4,1)S(1)}, s32[]{:S(2)}) async-start(s8[8388608]{0:T(1024)(128)(4,1)} %bitcast.80), calls=%async_computation.3 | async-start | bytes 8388608
  58.0 20.4 %collective-permute-start.3 = (f32[4,12,2,1024]{3,2,1,0:T(2,128)S(1)}, f32[4,12,2,1024]{3,2,1,0:T(2,128)}, u32[]{:S(2)}, u32[]{:S(2)}) collective-permute-start(f32[4,12,2,1024]{3,2,1,0:T(2,128)S(1)} %get-tuple-element.10), channel_id=1, source_target_pairs={{0,1},{1,2},{2,3},{3,4},{4,5},{5,6},{6,7},{8,9},{9,10},{10,11},{11... | collective-permute-start | bytes 1179656 | tf_op jit(solution)/shard_map/ppermute | solution.py:14
where the time goes:
time: 419 us; the launch traced here: 418 us
  blocking collectives  158 us (38%)
  matrix products  91.4 us (22%)
  local copies, waits for them, and re-layouts  66.6 us (16%)
  other arithmetic  60.2 us (14%)
  waiting for transfers between devices  28.9 us (7%)
  starting transfers between devices  13.2 us (3%)
    all_to_all x1, blocking collectives, local(): lax.all_to_all(solved, 'rad', split_axis=3, concat_axis=2, tiled=True)  81.7 us
    all_to_all x1, blocking collectives, local(): lax.all_to_all(radial(lax.all_to_all(solved, 'rad', split_axis=3, concat_...  76 us
    dot_general x1, matrix products, local(): jnp.einsum('cars,ts->cart', rhs, az_inverse, precision=lax.Precision.HIGH...  68.5 us
    unnamed x26, local copies, waits for them, and re-layouts  26.6 us
    dot_general x1, matrix products, radial(): jnp.einsum('rk,cakt->cart', rad_inverse, field, precision=lax.Precision.H...  23 us
    ppermute x2, waiting for transfers between devices, padded_2(): lax.ppermute(lax.slice_in_dim(block, 0, width, axis=dim), axis, backward)  21 us
    all_to_all x1, other arithmetic, local(): lax.all_to_all(solved, 'rad', split_axis=3, concat_axis=2, tiled=True)  19.5 us
    concatenate x5, other arithmetic, local(): fields = jnp.concatenate([velocity, viscosity[None]], axis=0)  18.3 us
  transfers between devices with their start and end apart: 4, of which 3 were waited for; matrix products, arithmetic and copies ran while one was open for 7% of the time, Pallas kernels for 0%

commit v1 on v0

--- a/solution.py
+++ b/solution.py
@@ -64,7 +64,14 @@
 
     solved = jnp.einsum("cars,ts->cart", rhs, az_inverse, precision=lax.Precision.HIGHEST)
     return lax.all_to_all(
-        radial(lax.all_to_all(solved, "rad", split_axis=3, concat_axis=2, tiled=True)),
+        radial(
+            jnp.concatenate(
+                lax.all_to_all(
+                    jnp.stack(jnp.split(solved, lax.axis_size("rad"), axis=3)), "rad", 0, 0
+                ),
+                axis=2,
+            )
+        ),
         "rad",
         split_axis=2,
         concat_axis=3,

time: 419 us -> 365 us (0.87); the launches traced: 418 us -> 358 us
  local copies, waits for them, and re-layouts: 66.6 us -> 32.4 us
  other arithmetic: 60.2 us -> 40 us
  waiting for transfers between devices: 28.9 us -> 24.3 us
    ppermute x2, waiting for transfers between devices: 21 us -> 1.1 us  [padded_2(): lax.ppermute(lax.slice_in_dim(block, 0, width, axis=dim), axis, backward)]
    all_to_all x1 -> x0, other arithmetic: 19.5 us -> none  [local(): lax.all_to_all(solved, 'rad', split_axis=3, concat_axis=2, tiled=True)]
    unnamed x26 -> x31, local copies, waits for them, and re-layouts: 26.6 us -> 10.2 us
    ppermute x2, waiting for transfers between devices: 7.97 us -> 23.2 us  [padded_2(): lax.ppermute(lax.slice_in_dim(block, block.shape[dim] - width, None, axis...]
    all_to_all x4 -> x2, local copies, waits for them, and re-layouts: 23.7 us -> 13.4 us  [local(): lax.all_to_all(radial(jnp.concatenate(lax.all_to_all(jnp.stack(jnp.split(...]
    dot_general x1 -> x0, local copies, waits for them, and re-layouts: 9.76 us -> none  [local(): jnp.einsum('cars,ts->cart', rhs, az_inverse, precision=lax.Precision.HIGH...]
  transfers between devices with their start and end apart: 4 -> 4, of which waited for: 3 -> 3; matrix products, arithmetic and copies ran while one was open for 7% -> 8% of each run, Pallas kernels for 0% -> 0%
where the time goes in v1:
time: 365 us; the launch traced here: 358 us
  blocking collectives  155 us (42%)
  matrix products  91 us (25%)
  other arithmetic  40 us (11%)
  local copies, waits for them, and re-layouts  32.4 us (9%)
  waiting for transfers between devices  24.3 us (7%)
  starting transfers between devices  15 us (4%)
    all_to_all x1, blocking collectives, local(): lax.all_to_all(jnp.stack(jnp.split(solved, lax.axis_size('rad'), axis=3))...  80.5 us
    all_to_all x1, blocking collectives, local(): lax.all_to_all(radial(jnp.concatenate(lax.all_to_all(jnp.stack(jnp.split(...  74.9 us
    dot_general x1, matrix products, local(): jnp.einsum('cars,ts->cart', rhs, az_inverse, precision=lax.Precision.HIGH...  68.3 us
    ppermute x2, waiting for transfers between devices, padded_2(): lax.ppermute(lax.slice_in_dim(block, block.shape[dim] - width, None, axis...  23.2 us
    dot_general x1, matrix products, radial(): jnp.einsum('rk,cakt->cart', rad_inverse, field, precision=lax.Precision.H...  22.7 us
    concatenate x5, other arithmetic, local(): fields = jnp.concatenate([velocity, viscosity[None]], axis=0)  18 us
    all_to_all x2, local copies, waits for them, and re-layouts, local(): lax.all_to_all(radial(jnp.concatenate(lax.all_to_all(jnp.stack(jnp.split(...  13.4 us
    unnamed x31, local copies, waits for them, and re-layouts  10.2 us
  transfers between devices with their start and end apart: 4, of which 3 were waited for; matrix products, arithmetic and copies ran while one was open for 8% of the time, Pallas kernels for 0%

profile of v1, /device:TPU:96, one launch (start us, length us, event | category | flops | bytes accessed | tf_op | source)
XLA Modules:
  0.0 358.2 jit_solution(12857092898732689098)
XLA Ops:
  0.0 0.0 copy-start
  0.0 0.0 copy-start.9
  0.0 0.0 copy-start.7
  0.0 0.0 copy-start.8
  0.0 0.0 copy-start.1
  0.0 0.0 copy-start.2
  0.0 5.0 %fusion.75 = (f32[4,2,64,1024]{3,2,1,0:T(8,128)}, f32[4,2,64,1024]{3,2,1,0:T(8,128)}) fusion(f32[3,8,64,1024]{3,2,1,0:T(8,128)} %param.7, f32[1,8,64,1024]{3,2,1,0:T(8,128)} %bitcast.96), kind=kLoop, calls=%fused_computation.109 | loop fusion | flops 1048576 | bytes 12582912 | tf_op jit(solution)/shard_map/concatenate | solution.py:58
  5.1 2.0 collective-permute-start.1
  7.1 4.5 %collective-permute-start = (f32[4,2,64,1024]{3,2,1,0:T(8,128)}, f32[4,2,64,1024]{3,2,1,0:T(8,128)}, u32[]{:S(2)}, u32[]{:S(2)}) collective-permute-start(f32[4,2,64,1024]{3,2,1,0:T(8,128)} %get-tuple-element.20), channel_id=1, source_target_pairs={{8,0},{16,8},{24,16},{32,24},{40,32},{48,40},{56,48},{64,56},{72,6... | collective-permute-start | bytes 6291464 | tf_op jit(solution)/shard_map/ppermute | solution.py:17
  11.7 0.0 copy-done.9
  11.7 0.0 copy-done.7
  11.7 0.6 mul.197
  12.3 0.0 copy-done.8
  12.3 0.5 mul.188
  12.8 0.0 copy-done.1
  12.8 0.0 copy-done.2
  12.8 1.7 fusion.91
  14.5 0.4 fusion.89
  14.9 0.0 copy-start.6
  14.9 0.0 copy-start.5
  15.0 5.2 %fusion.2 = f32[4,8,64,1022]{3,2,1,0:T(8,128)} fusion(f32[3,8,64,1024]{3,2,1,0:T(8,128)S(1)} %copy-done.1, f32[1,8,64,1024]{3,2,1,0:T(8,128)S(1)} %bitcast.99), kind=kLoop, calls=%fused_computation.22 | loop fusion | flops 2093056 | bytes 16760832 | tf_op jit(solution)/shard_map/concatenate | solution.py:58
  20.1 5.7 %fusion = (f32[4,8,64,1023]{3,2,1,0:T(8,128)S(1)}, f32[4,8,64,1023]{3,2,1,0:T(8,128)}) fusion(f32[3,8,64,1024]{3,2,1,0:T(8,128)S(1)} %copy-done.1, f32[1,8,64,1024]{3,2,1,0:T(8,128)S(1)} %bitcast.100), kind=kLoop, calls=%fused_computation.20 | loop fusion | flops 4190208 | bytes 25149440 | tf_op jit(solution)/shard_map/concatenate | solution.py:58
  25.8 0.0 copy-start.3
  25.8 0.0 copy-done.6
  25.8 2.1 fusion.83
  27.9 1.8 copy-done.3
  29.7 2.8 multiply_bitcast_fusion.2
  32.5 20.8 %collective-permute-done.1 = f32[4,2,64,1024]{3,2,1,0:T(8,128)S(1)} collective-permute-done((f32[4,2,64,1024]{3,2,1,0:T(8,128)}, f32[4,2,64,1024]{3,2,1,0:T(8,128)S(1)}, u32[]{:S(2)}, u32[]{:S(2)}) %collective-permute-start.1) | collective-permute-done | bytes 2097184 | tf_op jit(solution)/shard_map/ppermute | solution.py:14
  53.3 0.0 copy-start.4
  53.3 1.1 collective-permute-done
  54.4 1.4 pad_maximum_fusion.32
  55.8 1.3 collective-permute-start.2
  57.1 0.0 slice-start
  57.1 0.0 slice-start.1
  57.1 7.1 %collective-permute-start.3 = (f32[4,12,2,1024]{3,2,1,0:T(2,128)S(1)}, f32[4,12,2,1024]{3,2,1,0:T(2,128)}, u32[]{:S(2)}, u32[]{:S(2)}) collective-permute-start(f32[4,12,2,1024]{3,2,1,0:T(2,128)S(1)} %get-tuple-element.10), channel_id=1, source_target_pairs={{0,1},{1,2},{2,3},{3,4},{4,5},{5,6},{6,7},{8,9},{9,10},{10,11},{11... | collective-permute-start | bytes 1179656 | tf_op jit(solution)/shard_map/ppermute | solution.py:14
  64.2 0.0 copy-done.4
  64.2 8.5 %pad_maximum_fusion = (f32[4,10,64,1024]{3,2,1,0:T(8,128)}, f32[4,10,64,1024]{3,2,1,0:T(8,128)}) fusion(f32[4,2,64,1024]{3,2,1,0:T(8,128)} %collective-permute-done, f32[1,8,64,1024]{3,2,1,0:T(8,128)S(1)} %bitcast.102, f32[3,8,64,1024]{3,2,1,0:T(8,128)S(1)} %copy-done.1, f32[4,2,64,1024]{3,2,1,0:T(8,128)S(1)} %collective-permute-done.1), kind=kLoop, calls=%fused_computation.18 | loop fusion | flops 10485760 | bytes 33554432 | tf_op jit(solution)/shard_map/concatenate | solution.py:18
  72.7 0.0 collective-permute-done.2
  72.7 2.3 collective-permute-done.3
  75.1 0.0 copy-done.5
  75.1 0.0 slice-done
  75.1 0.0 slice-done.1
  75.1 6.1 %fusion.79 = (f32[8,64,1024]{2,1,0:T(8,128)}, f32[8,64,1024]{2,1,0:T(8,128)}, f32[8,64,1024]{2,1,0:T(8,128)}, f32[8,64,1024]{2,1,0:T(8,128)}, f32[8,64,1024]{2,1,0:T(8,128)}) fusion(f32[8,64,1024]{2,1,0:T(8,128)S(1)} %copy-done.2, f32[4,12,2,1024]{3,2,1,0:T(2,128)S(1)} %collective-permute-done.2, f32[4,2,64,1024]{3,2,1,0:T(8,128)} %collective-permute-done, ...), kind=kLoop, calls=%fused_computation.115 | loop fusion | flops 12058624 | bytes 34340864 | tf_op jit(solution)/shard_map/mul | solution.py:40
  81.2 68.3 %fusion.11 = f32[3,8,64,1024]{3,2,1,0:T(8,128)} fusion(f32[3,8,64,1024]{3,2,1,0:T(8,128)} %param.7, f32[4,12,2,1024]{3,2,1,0:T(2,128)} %collective-permute-done.3, f32[4,2,64,1024]{3,2,1,0:T(8,128)} %collective-permute-done, f32[4,2,64,1024]{3,2,1,0:T(8,128)} %copy-done.4, f32[1,8,64,1024]{3,2,1,0:T(8,128)S(1)} %bitcast.104, ...), kind=kOutput, calls=%fused_computation.32 | convolution fusion | flops 19428016128 | bytes 97257024 | tf_op jit(solution)/shard_map/cars,ts->cart/dot_general | solution.py:65
  149.5 1.2 fusion.100
  150.7 1.2 fusion.99
  151.9 1.2 fusion.98
  153.1 1.2 fusion.97
  154.3 1.2 fusion.96
  155.4 1.2 fusion.95
  156.6 1.2 fusion.94
  157.8 1.2 fusion.93
  159.0 80.5 %all_to_all.23 = f32[8,3,8,64,128]{4,3,2,1,0:T(8,128)S(1)} all-to-all(f32[8,3,8,64,128]{4,3,2,1,0:T(8,128)S(1)} %fusion.93), channel_id=1, replica_groups=mesh['ax'=16,'rad'=8] {'rad'}, dimensions={0} | all-to-all | bytes 12582912 | tf_op jit(solution)/shard_map/all_to_all | solution.py:69
  239.5 1.1 copy.16
  240.6 0.0 copy-done
  240.6 22.7 %convolution_bitcast_fusion = f32[3,8,512,128]{2,3,1,0:T(8,128)} fusion(f32[3,8,512,128]{3,2,1,0:T(8,128)S(1)} %bitcast.109, f32[512,512]{1,0:T(8,128)S(1)} %copy-done), kind=kOutput, calls=%fused_computation.107 | convolution fusion | flops 9663676416 | bytes 13631488 | tf_op jit(solution)/shard_map/rk,cakt->cart/dot_general | solution.py:63
  263.4 6.6 %copy.18 = f32[3,8,512,128]{3,1,0,2:T(8,128)} copy(f32[3,8,512,128]{2,3,1,0:T(8,128)} %convolution_bitcast_fusion) | data formatting | bytes 12582912 | tf_op jit(solution)/shard_map/rk,cakt->cart/transpose | solution.py:63
  270.0 74.9 %all_to_all.24 = f32[3,8,512,128]{3,1,0,2:T(8,128)S(1)} all-to-all(f32[3,8,512,128]{3,1,0,2:T(8,128)} %copy.18), channel_id=1, replica_groups=mesh['ax'=16,'rad'=8] {'rad'}, dimensions={2} | all-to-all | bytes 12582912 | tf_op jit(solution)/shard_map/all_to_all | solution.py:66
  344.9 6.3 %copy.20 = f32[3,8,64,8,128]{4,3,2,1,0:T(8,128)} copy(f32[3,8,64,8,128]{4,1,0,2,3:T(8,128)S(1)} %bitcast.108) | data formatting | bytes 12582912 | tf_op jit(solution)/shard_map/all_to_all | solution.py:66
  351.2 7.1 %all_to_all.20 = f32[3,8,64,1024]{3,2,1,0:T(8,128)} reshape(f32[3,8,64,8,128]{4,3,2,1,0:T(8,128)} %copy.20) | data formatting | bytes 12582912 | tf_op jit(solution)/shard_map/all_to_all | solution.py:66
  (2 shorter events, 0.0 us)
Async XLA Ops:
  0.0 240.6 %copy-start = (f32[512,512]{1,0:T(8,128)S(1)}, f32[512,512]{1,0:T(8,128)}, u32[]{:S(2)}) copy-start(f32[512,512]{1,0:T(8,128)} %param.13) | copy-start | bytes 3145732
  0.0 11.7 %copy-start.9 = (f32[8]{0:T(128)S(1)}, f32[8]{0:T(128)}, u32[]{:S(2)}) copy-start(f32[8]{0:T(128)} %param.9) | copy-start | bytes 100
  0.0 11.7 %copy-start.7 = (f32[64]{0:T(128)S(1)}, f32[64]{0:T(128)}, u32[]{:S(2)}) copy-start(f32[64]{0:T(128)} %param.10) | copy-start | bytes 772
  0.0 12.3 %copy-start.8 = (f32[64]{0:T(128)S(1)}, f32[64]{0:T(128)}, u32[]{:S(2)}) copy-start(f32[64]{0:T(128)} %param.11) | copy-start | bytes 772
  0.0 12.8 %copy-start.1 = (f32[3,8,64,1024]{3,2,1,0:T(8,128)S(1)}, f32[3,8,64,1024]{3,2,1,0:T(8,128)}, u32[]{:S(2)}) copy-start(f32[3,8,64,1024]{3,2,1,0:T(8,128)} %param.7) | copy-start | bytes 18874372
  0.0 12.8 %copy-start.2 = (f32[8,64,1024]{2,1,0:T(8,128)S(1)}, f32[8,64,1024]{2,1,0:T(8,128)}, u32[]{:S(2)}) copy-start(f32[8,64,1024]{2,1,0:T(8,128)} %param.8) | copy-start | bytes 6291460
  5.1 48.3 %collective-permute-start.1 = (f32[4,2,64,1024]{3,2,1,0:T(8,128)}, f32[4,2,64,1024]{3,2,1,0:T(8,128)S(1)}, u32[]{:S(2)}, u32[]{:S(2)}) collective-permute-start(f32[4,2,64,1024]{3,2,1,0:T(8,128)} %get-tuple-element.19), channel_id=1, source_target_pairs={{0,8},{8,16},{16,24},{24,32},{32,40},{40,48},{48,56},{56,64},{64,7... | collective-permute-start | bytes 6291464 | tf_op jit(solution)/shard_map/ppermute | solution.py:14
  7.1 47.3 %collective-permute-start = (f32[4,2,64,1024]{3,2,1,0:T(8,128)}, f32[4,2,64,1024]{3,2,1,0:T(8,128)}, u32[]{:S(2)}, u32[]{:S(2)}) collective-permute-start(f32[4,2,64,1024]{3,2,1,0:T(8,128)} %get-tuple-element.20), channel_id=1, source_target_pairs={{8,0},{16,8},{24,16},{32,24},{40,32},{48,40},{56,48},{64,56},{72,6... | collective-permute-start | bytes 6291464 | tf_op jit(solution)/shard_map/ppermute | solution.py:17
  14.9 10.9 %copy-start.6 = (f32[4,8,64,1]{3,2,1,0:T(8,128)}, f32[4,8,64,1]{3,2,1,0:T(8,128)S(1)}, u32[]{:S(2)}) copy-start(f32[4,8,64,1]{3,2,1,0:T(8,128)S(1)} %get-tuple-element.13) | copy-start | bytes 24580
  14.9 60.1 %copy-start.5 = (f32[4,8,64,1]{3,2,1,0:T(8,128)}, f32[4,8,64,1]{3,2,1,0:T(8,128)S(1)}, u32[]{:S(2)}) copy-start(f32[4,8,64,1]{3,2,1,0:T(8,128)S(1)} %get-tuple-element.14) | copy-start | bytes 24580
  25.8 3.9 %copy-start.3 = (f32[4,8,64,1023]{3,2,1,0:T(8,128)}, f32[4,8,64,1023]{3,2,1,0:T(8,128)S(1)}, u32[]{:S(2)}) copy-start(f32[4,8,64,1023]{3,2,1,0:T(8,128)S(1)} %get-tuple-element.11) | copy-start | bytes 25141252
  53.3 10.9 %copy-start.4 = (f32[4,2,64,1024]{3,2,1,0:T(8,128)}, f32[4,2,64,1024]{3,2,1,0:T(8,128)S(1)}, u32[]{:S(2)}) copy-start(f32[4,2,64,1024]{3,2,1,0:T(8,128)S(1)} %collective-permute-done.1) | copy-start | bytes 6291460
  55.8 16.9 %collective-permute-start.2 = (f32[4,12,2,1024]{3,2,1,0:T(2,128)S(1)}, f32[4,12,2,1024]{3,2,1,0:T(2,128)S(1)}, u32[]{:S(2)}, u32[]{:S(2)}) collective-permute-start(f32[4,12,2,1024]{3,2,1,0:T(2,128)S(1)} %get-tuple-element.9), channel_id=1, source_target_pairs={{1,0},{2,1},{3,2},{4,3},{5,4},{6,5},{7,6},{9,8},{10,9},{11,10},{12... | collective-permute-start | bytes 1179656 | tf_op jit(solution)/shard_map/ppermute | solution.py:17
  57.1 17.9 %slice-start = ((s8[8388608]{0:T(1024)(128)(4,1)}), s8[4194304]{0:T(1024)(128)(4,1)S(1)}, s32[]{:S(2)}) async-start(s8[8388608]{0:T(1024)(128)(4,1)} %bitcast.105), calls=%async_computation.2 | async-start | bytes 8388608
  57.1 17.9 %slice-start.1 = ((s8[8388608]{0:T(1024)(128)(4,1)}), s8[4194304]{0:T(1024)(128)(4,1)S(1)}, s32[]{:S(2)}) async-start(s8[8388608]{0:T(1024)(128)(4,1)} %bitcast.105), calls=%async_computation.3 | async-start | bytes 8388608
  57.1 17.9 %collective-permute-start.3 = (f32[4,12,2,1024]{3,2,1,0:T(2,128)S(1)}, f32[4,12,2,1024]{3,2,1,0:T(2,128)}, u32[]{:S(2)}, u32[]{:S(2)}) collective-permute-start(f32[4,12,2,1024]{3,2,1,0:T(2,128)S(1)} %get-tuple-element.10), channel_id=1, source_target_pairs={{0,1},{1,2},{2,3},{3,4},{4,5},{5,6},{6,7},{8,9},{9,10},{10,11},{11... | collective-permute-start | bytes 1179656 | tf_op jit(solution)/shard_map/ppermute | solution.py:14
